TPU v7x, 256 devices: a whole 4x4x8 slice. The times are simulated.
256 devices in a mesh: rows: 64 (over y, z, core), rhs: 4 (over x).
Axes of the slice: x: 4, y: 4, z: 8, core: 2. Of those that a mesh axis runs over, the one named last changes fastest.
Arguments:
- right_side: bfloat16 [16, 64, 256, 128], P(None, 'rows', 'rhs'), may hold values from -6 to 6
- lower: bfloat16 [16, 64, 4, 128, 128], P(None, 'rows', 'rhs'), may hold values from -0.1875 to 0.1875
- diag_inv: bfloat16 [16, 64, 128, 128], P(None, 'rows'), may hold values from -0.5 to 0.5
- levels: int32 [16, 64], replicated, may hold values from 0 to 7, as said below
- columns: int32 [16, 64, 4], P(None, 'rows'), may hold values from -1 to 1023, as said below
Outputs:
- solved: bfloat16 [16, 64, 256, 128], P(None, 'rows', 'rhs')
Inputs may be any that keep to these rules, and one draw needn't show every extreme that they name: `levels`: every index of rows holds exactly 2 block rows of each level. `columns`: level 0 block rows hold only -1. A block row of level l > 0 holds no -1; its slot 0 names a block row of level l - 1, the other slots block rows of levels below l. The stored blocks of one index's block rows of one level name block rows of any one index of rows at most 1 times, and exactly 1 times for some index.
All inputs are finite; a program needn't handle non-finite values.
Results may differ from a plain program's by a relative error of at most 0.0085.
Values may be sent and summed in bfloat16 or wider, within the bound.
No kernel may reach another device: no remote copies, remote signals or barrier semaphores. Data moves between devices by JAX's collectives and lax.ppermute only.
A program may use at most 64 MiB of HBM per device.

v0:
```python
import jax
import jax.numpy as jnp
from jax import lax
from jax.sharding import PartitionSpec as P

LEVELS = 8


def local(right_side, lower, diag_inv, levels, columns):
    r_local = right_side.shape[0]
    width_rhs = right_side.shape[2]
    block = right_side.shape[3]
    count = lax.axis_size("rows")
    myself = lax.axis_index("rows")
    each = r_local // LEVELS
    level_table = levels.T
    order = jnp.argsort(level_table, axis=1, stable=True)
    rank = jnp.argsort(order, axis=1) % each
    mine = lax.dynamic_index_in_dim(order, myself, 0, keepdims=False)
    rhs_rows = right_side[:, 0]
    own_tiles = lower[:, 0]
    inverses = diag_inv[:, 0]
    column_of = columns[:, 0]
    tiles_all = lax.all_gather(own_tiles, "rhs", axis=1, tiled=True)
    store = jnp.zeros((LEVELS, count * each, width_rhs, block), jnp.bfloat16)
    solution = jnp.zeros_like(rhs_rows)
    for level in range(LEVELS):
        picked = mine[level * each : (level + 1) * each]
        partial_value = rhs_rows[picked].astype(jnp.float32)
        if level > 0:
            tiles = tiles_all[picked]
            wanted = column_of[picked]
            owner = wanted % count
            owner_row = wanted // count
            wanted_level = level_table[owner, owner_row]
            wanted_slot = owner * each + rank[owner, owner_row]
            known = store[wanted_level, wanted_slot]
            partial_value = partial_value - jnp.einsum(
                "rjcb,rjab->rca", known, tiles, preferred_element_type=jnp.float32
            )
        rounded = partial_value.astype(jnp.bfloat16)
        result = jnp.einsum(
            "rcb,rab->rca", rounded, inverses[picked], preferred_element_type=jnp.float32
        ).astype(jnp.bfloat16)
        solution = solution.at[picked].set(result)
        if level < LEVELS - 1:
            gathered = lax.all_gather(result, "rows", axis=0, tiled=True)
            store = store.at[level].set(gathered)
    return solution[:, None]


def solution(mesh):
    in_specs = (
        P(None, "rows", "rhs", None),
        P(None, "rows", "rhs", None, None),
        P(None, "rows", None, None),
        P(),
        P(None, "rows", None),
    )
    out_specs = P(None, "rows", "rhs", None)
    return jax.shard_map(local, mesh=mesh, in_specs=in_specs, out_specs=out_specs, check_vma=False)
```

profile of v0, /device:TPU:1, one launch (start us, length us, event | category | flops | bytes accessed | tf_op | source)
XLA Modules:
  0.0 662.2 jit_solution(14776794582719155596)
XLA Ops:
  19.2 27.2 %all-gather.24.cloned.1.call-done = bf16[16,4,1,128,128]{4,3,2,1,0:T(8,128)(2,1)} async-done(((bf16[16,1,1,128,128]{4,3,2,1,0:T(8,128)(2,1)}), bf16[16,4,1,128,128]{4,3,2,1,0:T(8,128)(2,1)}) %all-gather.24.cloned.1.call-update) | async-done | bytes 2097168 | tf_op jit(solution)/shard_map/all_gather | solution.py:24
  46.4 2.3 gather_fusion.7
  48.7 78.3 %all-gather.10.cloned.1.call-done = bf16[128,64,128]{2,1,0:T(8,128)(2,1)} async-done(((bf16[2,64,128]{2,1,0:T(8,128)(2,1)}), bf16[128,64,128]{2,1,0:T(8,128)(2,1)}) %all-gather.10.cloned.1.call-update) | async-done | bytes 2097168 | tf_op jit(solution)/shard_map/all_gather | solution.py:47
  127.0 7.1 %scatter.92 = bf16[8,128,64,128]{3,2,1,0:T(8,128)(2,1)} pad(bf16[1,128,64,128]{3,2,1,0:T(8,128)(2,1)} %bitcast.328, bf16[]{:T(256)} %constant.311.clone.1), padding=0_7x0_0x0_0x0_0 | pad | bytes 18874370 | tf_op jit(solution)/shard_map/scatter | solution.py:48
  134.1 6.4 gather_fusion.6
  145.8 70.8 %all-gather.12.cloned.1.call-done = bf16[128,64,128]{2,1,0:T(8,128)(2,1)} async-done(((bf16[2,64,128]{2,1,0:T(8,128)(2,1)}), bf16[128,64,128]{2,1,0:T(8,128)(2,1)}) %all-gather.12.cloned.1.call-update) | async-done | bytes 2097168 | tf_op jit(solution)/shard_map/all_gather | solution.py:47
  216.6 3.1 bitcast_dynamic-update-slice_fusion.5
  219.6 6.4 gather_fusion.13
  232.5 69.6 %all-gather.14.cloned.1.call-done = bf16[128,64,128]{2,1,0:T(8,128)(2,1)} async-done(((bf16[2,64,128]{2,1,0:T(8,128)(2,1)}), bf16[128,64,128]{2,1,0:T(8,128)(2,1)}) %all-gather.14.cloned.1.call-update) | async-done | bytes 2097168 | tf_op jit(solution)/shard_map/all_gather | solution.py:47
  302.1 3.1 bitcast_dynamic-update-slice_fusion.4
  305.2 6.4 gather_fusion.20
  314.5 1.5 gather_fusion.23
  316.9 70.8 %all-gather.16.cloned.1.call-done = bf16[128,64,128]{2,1,0:T(8,128)(2,1)} async-done(((bf16[2,64,128]{2,1,0:T(8,128)(2,1)}), bf16[128,64,128]{2,1,0:T(8,128)(2,1)}) %all-gather.16.cloned.1.call-update) | async-done | bytes 2097168 | tf_op jit(solution)/shard_map/all_gather | solution.py:47
  387.6 3.1 bitcast_dynamic-update-slice_fusion.3
  390.7 6.4 gather_fusion.27
  403.6 69.6 %all-gather.18.cloned.1.call-done = bf16[128,64,128]{2,1,0:T(8,128)(2,1)} async-done(((bf16[2,64,128]{2,1,0:T(8,128)(2,1)}), bf16[128,64,128]{2,1,0:T(8,128)(2,1)}) %all-gather.18.cloned.1.call-update) | async-done | bytes 2097168 | tf_op jit(solution)/shard_map/all_gather | solution.py:47
  473.2 3.2 bitcast_dynamic-update-slice_fusion.2
  476.3 6.4 gather_fusion.34
  488.0 70.8 %all-gather.20.cloned.1.call-done = bf16[128,64,128]{2,1,0:T(8,128)(2,1)} async-done(((bf16[2,64,128]{2,1,0:T(8,128)(2,1)}), bf16[128,64,128]{2,1,0:T(8,128)(2,1)}) %all-gather.20.cloned.1.call-update) | async-done | bytes 2097168 | tf_op jit(solution)/shard_map/all_gather | solution.py:47
  558.8 3.1 bitcast_dynamic-update-slice_fusion.1
  561.8 6.4 gather_fusion.41
  579.9 64.4 %all-gather.22.cloned.1.call-done = bf16[128,64,128]{2,1,0:T(8,128)(2,1)} async-done(((bf16[2,64,128]{2,1,0:T(8,128)(2,1)}), bf16[128,64,128]{2,1,0:T(8,128)(2,1)}) %all-gather.22.cloned.1.call-update) | async-done | bytes 2097168 | tf_op jit(solution)/shard_map/all_gather | solution.py:47
  644.3 3.1 bitcast_dynamic-update-slice_fusion
  647.4 6.4 gather_fusion.48
  (156 shorter events, 53.0 us)
Async XLA Ops:
  6.5 2.5 copy-start
  6.5 135.7 %copy-start.1 = (s32[16,64]{1,0:T(8,128)S(1)}, s32[16,64]{1,0:T(8,128)}, u32[]{:S(2)}) copy-start(s32[16,64]{1,0:T(8,128)} %param.22) | copy-start | bytes 12292
  6.5 39.8 %all-gather.24.cloned.1.call-start = ((), (), s32[]{:S(2)}) async-start(), calls=%async_computation.7 | async-start | bytes 2621440 | tf_op jit(solution)/shard_map/all_gather | solution.py:24
  7.3 119.7 %all-gather.10.cloned.1.call-start = ((), (), s32[]{:S(2)}) async-start(), calls=%async_computation | async-start | bytes 2129920 | tf_op jit(solution)/shard_map/all_gather | solution.py:47
  11.9 204.6 %all-gather.12.cloned.1.call-start = ((), (), s32[]{:S(2)}) async-start(), calls=%async_computation.1 | async-start | bytes 2129920 | tf_op jit(solution)/shard_map/all_gather | solution.py:47
  46.4 98.8 %copy-start.2 = (bf16[16,4,1,128,128]{4,3,2,1,0:T(8,128)(2,1)S(1)}, bf16[16,4,1,128,128]{4,3,2,1,0:T(8,128)(2,1)}, u32[]{:S(2)}) copy-start(bf16[16,4,1,128,128]{4,3,2,1,0:T(8,128)(2,1)} %all-gather.24.cloned.1.call-done) | copy-start | bytes 6291460
  141.4 160.6 %all-gather.14.cloned.1.call-start = ((), (), s32[]{:S(2)}) async-start(), calls=%async_computation.2 | async-start | bytes 2129920 | tf_op jit(solution)/shard_map/all_gather | solution.py:47
  226.9 160.7 %all-gather.16.cloned.1.call-start = ((), (), s32[]{:S(2)}) async-start(), calls=%async_computation.3 | async-start | bytes 2129920 | tf_op jit(solution)/shard_map/all_gather | solution.py:47
  228.9 344.6 %copy-start.8 = (bf16[2,64,128]{2,1,0:T(8,128)(2,1)S(1)}, bf16[2,64,128]{2,1,0:T(8,128)(2,1)}, u32[]{:S(2)}) copy-start(bf16[2,64,128]{2,1,0:T(8,128)(2,1)} %convolution_convert_fusion.7) | copy-start | bytes 98308
  228.9 345.8 %copy-start.4 = (bf16[2,64,128]{2,1,0:T(8,128)(2,1)S(1)}, bf16[2,64,128]{2,1,0:T(8,128)(2,1)}, u32[]{:S(2)}) copy-start(bf16[2,64,128]{2,1,0:T(8,128)(2,1)} %convolution_convert_fusion.6) | copy-start | bytes 98308
  228.9 346.4 %copy-start.5 = (bf16[2,64,128]{2,1,0:T(8,128)(2,1)S(1)}, bf16[2,64,128]{2,1,0:T(8,128)(2,1)}, u32[]{:S(2)}) copy-start(bf16[2,64,128]{2,1,0:T(8,128)(2,1)} %convolution_convert_fusion.5) | copy-start | bytes 98308
  312.5 263.5 %copy-start.6 = (bf16[2,64,128]{2,1,0:T(8,128)(2,1)S(1)}, bf16[2,64,128]{2,1,0:T(8,128)(2,1)}, u32[]{:S(2)}) copy-start(bf16[2,64,128]{2,1,0:T(8,128)(2,1)} %convolution_convert_fusion.4) | copy-start | bytes 98308
  312.5 160.7 %all-gather.18.cloned.1.call-start = ((), (), s32[]{:S(2)}) async-start(), calls=%async_computation.4 | async-start | bytes 2129920 | tf_op jit(solution)/shard_map/all_gather | solution.py:47
  398.0 178.6 %copy-start.7 = (bf16[2,64,128]{2,1,0:T(8,128)(2,1)S(1)}, bf16[2,64,128]{2,1,0:T(8,128)(2,1)}, u32[]{:S(2)}) copy-start(bf16[2,64,128]{2,1,0:T(8,128)(2,1)} %convolution_convert_fusion.3) | copy-start | bytes 98308
  398.0 160.7 %all-gather.20.cloned.1.call-start = ((), (), s32[]{:S(2)}) async-start(), calls=%async_computation.5 | async-start | bytes 2129920 | tf_op jit(solution)/shard_map/all_gather | solution.py:47
  483.6 160.6 %all-gather.22.cloned.1.call-start = ((), (), s32[]{:S(2)}) async-start(), calls=%async_computation.6 | async-start | bytes 2129920 | tf_op jit(solution)/shard_map/all_gather | solution.py:47
  654.7 0.7 copy-start.3
Sparse Core Ops, SparseCore 0:
  9.2 37.1 all-gather.23
  49.1 77.7 all-gather.9
  141.6 74.9 all-gather.11
  227.1 74.9 all-gather.13
  312.6 74.9 all-gather.15
  398.1 74.9 all-gather.17
  483.7 74.9 all-gather.19
  569.2 74.9 all-gather.21
where the time goes:
time: 663 us; the launch traced here: 662 us
  waiting for transfers between devices  522 us (79%)
  local copies, waits for them, and re-layouts  117 us (18%)
  between operations  13.9 us (2%)
  matrix products  6.68 us (1%)
    all_gather x7, waiting for transfers between devices, local(): gathered = lax.all_gather(result, 'rows', axis=0, tiled=True)  494 us
    gather x7, local copies, waits for them, and re-layouts, local(): known = store[wanted_level, wanted_slot]  44.5 us
    all_gather x1, waiting for transfers between devices, local(): tiles_all = lax.all_gather(own_tiles, 'rhs', axis=1, tiled=True)  27.2 us
    scatter x7, local copies, waits for them, and re-layouts, local(): store = store.at[level].set(gathered)  25.7 us
  transfers between devices with their start and end apart: 8, of which 8 were waited for; matrix products, arithmetic and copies ran while one was open for 7% of the time, Pallas kernels for 0%

commit v1 on v0

v1 whole, which is shorter than its diff:
```python
import functools

import jax
import jax.numpy as jnp
from jax import lax
from jax.experimental import pallas as pl
from jax.experimental.pallas import tpu as pltpu
from jax.sharding import PartitionSpec as P

LEVELS = 8
EACH = 2
NNZ = 4
Y, Z, C = 4, 8, 2


def swap(x, mask):
    return lax.ppermute(x, "rows", [(i, i ^ mask) for i in range(Y * Z * C)])


def exchange(x):
    line = jnp.concatenate([x] + [swap(x, d << 1) for d in range(1, Z)], 0)
    plane = jnp.concatenate([line] + [swap(line, e << 4) for e in range(1, Y)], 0)
    return plane, swap(plane, 1)


def level_kernel(level, plan, *refs):
    n_known = 2 * level
    known = refs[:n_known]
    rhs, inverse = refs[n_known : n_known + 2]
    at = n_known + 2
    tiles = None
    if level > 0:
        tiles = refs[at]
        at += 2
    fresh, solved, rhs_buf, inv_buf, out_buf, sems = refs[at : at + 6]
    known_buf, tile_buf, known_sems, tile_sems = refs[at + 6 : at + 10] if level > 0 else (None,) * 4

    rows = [plan[level * EACH + m] for m in range(EACH)]
    first = []
    for m in range(EACH):
        if level > 0:
            for j in range(NNZ):
                s = m * NNZ + j
                code = plan[LEVELS * EACH + (level * EACH + m) * NNZ + j]
                which = code // 256
                place = code % 256
                for k in range(n_known):

                    @pl.when(which == k)
                    def _(k=k, s=s, place=place):
                        pltpu.make_async_copy(known[k].at[place], known_buf.at[s], known_sems.at[s]).start()

            pltpu.make_async_copy(tiles.at[rows[m]], tile_buf.at[m], tile_sems.at[m]).start()
        c1 = pltpu.make_async_copy(rhs.at[rows[m]], rhs_buf.at[m], sems.at[m])
        c2 = pltpu.make_async_copy(inverse.at[rows[m]], inv_buf.at[m], sems.at[EACH + m])
        c1.start()
        c2.start()
        first.append((c1, c2))
    outs = []
    for m in range(EACH):
        first[m][0].wait()
        total = rhs_buf[m].astype(jnp.float32)
        if level > 0:
            pltpu.make_async_copy(tiles.at[rows[m]], tile_buf.at[m], tile_sems.at[m]).wait()
            for j in range(NNZ):
                s = m * NNZ + j
                pltpu.make_async_copy(known[0].at[0], known_buf.at[s], known_sems.at[s]).wait()
                total = total - lax.dot_general(
                    known_buf[s], tile_buf[m, j], (((1,), (1,)), ((), ())), preferred_element_type=jnp.float32
                )
        first[m][1].wait()
        x = lax.dot_general(
            total.astype(jnp.bfloat16), inv_buf[m], (((1,), (1,)), ((), ())), preferred_element_type=jnp.float32
        ).astype(jnp.bfloat16)
        fresh[m] = x
        out_buf[m] = x
        c = pltpu.make_async_copy(out_buf.at[m], solved.at[rows[m]], sems.at[2 * EACH + m])
        c.start()
        outs.append(c)
    for c in outs:
        c.wait()


def solve_level(level, plan, known, rhs, inverse, tiles, solved):
    n, width, block = rhs.shape
    kind = rhs.dtype
    any_spec = pl.BlockSpec(memory_space=pl.ANY)
    operands = [plan, *known, rhs, inverse]
    scratch = [
        pltpu.VMEM((EACH, width, block), kind),
        pltpu.VMEM((EACH, block, block), kind),
        pltpu.VMEM((EACH, width, block), kind),
        pltpu.SemaphoreType.DMA((3 * EACH,)),
    ]
    aliases = {}
    if level > 0:
        operands += [tiles, solved]
        aliases = {len(operands) - 1: 1}
        scratch += [
            pltpu.VMEM((EACH * NNZ, width, block), kind),
            pltpu.VMEM((EACH, NNZ, block, block), kind),
            pltpu.SemaphoreType.DMA((EACH * NNZ,)),
            pltpu.SemaphoreType.DMA((EACH,)),
        ]
    return pl.pallas_call(
        functools.partial(level_kernel, level),
        out_shape=(jax.ShapeDtypeStruct((EACH, width, block), kind), jax.ShapeDtypeStruct(rhs.shape, kind)),
        in_specs=[pl.BlockSpec(memory_space=pltpu.SMEM)] + [any_spec] * (len(operands) - 1),
        out_specs=(pl.BlockSpec(memory_space=pltpu.VMEM), any_spec),
        scratch_shapes=scratch,
        input_output_aliases=aliases,
        name=f"level_{level}",
    )(*operands)


def make_plan(levels, column_of, me):
    n = levels.shape[0]
    row = jnp.arange(n, dtype=jnp.int32)
    earlier = row[None, :] < row[:, None]
    same = levels[:, None, :] == levels[None, :, :]
    rank = jnp.sum(jnp.where(same & earlier[:, :, None], 1, 0), 1)
    spot = levels * EACH + rank
    mine = lax.dynamic_index_in_dim(spot, me, 1, keepdims=False)
    hit = mine[None, :] == row[:, None]
    order = jnp.sum(jnp.where(hit, row[None, :], 0), 1)
    wanted = jnp.sum(jnp.where(hit[:, :, None], column_of[None], 0), 1).reshape(-1)
    everyone = jnp.arange(spot.size, dtype=jnp.int32)
    found = jnp.sum(jnp.where(wanted[:, None] == everyone[None, :], spot.reshape(-1)[None, :], 0), 1)
    apart = (wanted % (Y * Z * C)) ^ me
    code = (found // EACH * C + apart % C) * 256 + apart // C * EACH + found % EACH
    return jnp.concatenate([order, code])


def local(right_side, lower, diag_inv, levels, columns):
    me = lax.axis_index("rows")
    rhs = right_side[:, 0]
    inverse = diag_inv[:, 0]
    plan = make_plan(levels, columns[:, 0], me)
    tiles = lax.all_gather(lower[:, 0], "rhs", axis=1, tiled=True)
    known, solved = [], None
    for level in range(LEVELS):
        fresh, solved = solve_level(level, plan, known, rhs, inverse, tiles, solved)
        if level < LEVELS - 1:
            known += exchange(fresh)
    return solved[:, None]


def solution(mesh):
    in_specs = (
        P(None, "rows", "rhs", None),
        P(None, "rows", "rhs", None, None),
        P(None, "rows", None, None),
        P(),
        P(None, "rows", None),
    )
    out_specs = P(None, "rows", "rhs", None)
    return jax.shard_map(local, mesh=mesh, in_specs=in_specs, out_specs=out_specs, check_vma=False)
```

time: 663 us -> 340 us (0.51)
  waiting for transfers between devices: 522 us -> 125 us
  starting transfers between devices: 0.29 us -> 142 us
  local copies, waits for them, and re-layouts: 117 us -> 14.7 us
  Pallas kernels: 0 us -> 35.6 us
  matrix products: 6.68 us -> 0 us
    all_gather x8 -> x1, waiting for transfers between devices: 521 us -> 0.01 us  [local(): tiles = lax.all_gather(lower[:, 0], 'rhs', axis=1, tiled=True)]
    ppermute x0 -> x77, starting transfers between devices: none -> 142 us  [swap(): return lax.ppermute(x, 'rows', [(i, i ^ mask) for i in range(Y * Z * C)])]
    ppermute x0 -> x77, waiting for transfers between devices: none -> 124 us  [swap(): return lax.ppermute(x, 'rows', [(i, i ^ mask) for i in range(Y * Z * C)])]
    gather x65 -> x0, local copies, waits for them, and re-layouts: 81.7 us -> none  [the longest x7 44.5 us: local(): known = store[wanted_level, wanted_slot]]
    pallas_call x0 -> x8, Pallas kernels: none -> 35.6 us  [solve_level(): pl.pallas_call(functools.partial(level_kernel, level), out_shape=(jax.Sha...]
    scatter x15 -> x0, local copies, waits for them, and re-layouts: 32 us -> none  [the longest x7 25.7 us: local(): store = store.at[level].set(gathered)]
    unnamed x18 -> x91, local copies, waits for them, and re-layouts: 0.73 us -> 13.9 us
    dot_general x8 -> x0, matrix products: 6.68 us -> none  [local(): jnp.einsum('rcb,rab->rca', rounded, inverses[picked], preferred_element_t...]
  transfers between devices with their start and end apart: 8 -> 78, of which waited for: 8 -> 44; matrix products, arithmetic and copies ran while one was open for 7% -> 3% of each run, Pallas kernels for 0% -> 1%
where the time goes in v1:
time: 340 us; the launch traced here: 335 us
  starting transfers between devices  142 us (42%)
  waiting for transfers between devices  125 us (37%)
  Pallas kernels  35.6 us (10%)
  local copies, waits for them, and re-layouts  14.7 us (4%)
  between operations  14.3 us (4%)
    ppermute x77, starting transfers between devices, swap(): return lax.ppermute(x, 'rows', [(i, i ^ mask) for i in range(Y * Z * C)])  142 us
    ppermute x77, waiting for transfers between devices, swap(): return lax.ppermute(x, 'rows', [(i, i ^ mask) for i in range(Y * Z * C)])  124 us
    pallas_call x8, Pallas kernels, solve_level(): pl.pallas_call(functools.partial(level_kernel, level), out_shape=(jax.Sha...  35.6 us
    unnamed x91, local copies, waits for them, and re-layouts  13.9 us
  transfers between devices with their start and end apart: 78, of which 44 were waited for; matrix products, arithmetic and copies ran while one was open for 3% of the time, Pallas kernels for 1%

profile of v1, /device:TPU:1, one launch (start us, length us, event | category | flops | bytes accessed | tf_op | source)
XLA Modules:
  0.0 334.5 jit_solution(12851090566888387298)
XLA Ops:
  19.6 5.8 %collective-permute-start.3 = (bf16[2,64,128]{2,1,0:T(8,128)(2,1)}, bf16[2,64,128]{2,1,0:T(8,128)(2,1)S(1)}, u32[]{:S(2)}, u32[]{:S(2)}) collective-permute-start(bf16[2,64,128]{2,1,0:T(8,128)(2,1)} %get-tuple-element.20), channel_id=1, source_target_pairs={{0,32},{4,36},{8,40},{12,44},{16,48},{20,52},{24,56},{28,60},{32,0... | collective-permute-start | bytes 98312 | tf_op jit(solution)/shard_map/ppermute | solution.py:17
  26.3 4.1 %collective-permute-start.5 = (bf16[2,64,128]{2,1,0:T(8,128)(2,1)}, bf16[2,64,128]{2,1,0:T(8,128)(2,1)S(1)}, u32[]{:S(2)}, u32[]{:S(2)}) collective-permute-start(bf16[2,64,128]{2,1,0:T(8,128)(2,1)} %get-tuple-element.20), channel_id=1, source_target_pairs={{0,48},{4,52},{8,56},{12,60},{16,32},{20,36},{24,40},{28,44},{32,1... | collective-permute-start | bytes 98312 | tf_op jit(solution)/shard_map/ppermute | solution.py:17
  40.9 6.8 %collective-permute-done.8 = bf16[16,64,128]{2,1,0:T(8,128)(2,1)S(1)} collective-permute-done((bf16[16,64,128]{2,1,0:T(8,128)(2,1)S(1)}, bf16[16,64,128]{2,1,0:T(8,128)(2,1)S(1)}, u32[]{:S(2)}, u32[]{:S(2)}) %collective-permute-start.8) | collective-permute-done | bytes 262176 | tf_op jit(solution)/shard_map/ppermute | solution.py:17
  47.7 4.8 %collective-permute-done.9 = bf16[16,64,128]{2,1,0:T(8,128)(2,1)S(1)} collective-permute-done((bf16[16,64,128]{2,1,0:T(8,128)(2,1)S(1)}, bf16[16,64,128]{2,1,0:T(8,128)(2,1)S(1)}, u32[]{:S(2)}, u32[]{:S(2)}) %collective-permute-start.9) | collective-permute-done | bytes 262176 | tf_op jit(solution)/shard_map/ppermute | solution.py:17
  58.1 4.6 %level_1.1 = (bf16[2,64,128]{2,1,0:T(8,128)(2,1)}, bf16[16,64,128]{2,1,0:T(8,128)(2,1)}) custom-call(s32[80]{0:T(128)} %pad_add_fusion.plan, bf16[64,64,128]{2,1,0:T(8,128)(2,1)} %copy-done, bf16[64,64,128]{2,1,0:T(8,128)(2,1)} %copy-done.1, bf16[16,64,128]{2,1,0:T(8,128)(2,1)} %bitcast.24, ...), custom_call_target="tpu_custom_call", output_to_operand_aliasing={{1}: (6, {})} | custom-call | tf_op jit(solution)/shard_map/level_1/pallas_call | solution.py:105
  83.2 4.9 %collective-permute-done.19 = bf16[16,64,128]{2,1,0:T(8,128)(2,1)S(1)} collective-permute-done((bf16[16,64,128]{2,1,0:T(8,128)(2,1)S(1)}, bf16[16,64,128]{2,1,0:T(8,128)(2,1)S(1)}, u32[]{:S(2)}, u32[]{:S(2)}) %collective-permute-start.19) | collective-permute-done | bytes 262176 | tf_op jit(solution)/shard_map/ppermute | solution.py:17
  88.2 4.5 %collective-permute-done.20 = bf16[16,64,128]{2,1,0:T(8,128)(2,1)S(1)} collective-permute-done((bf16[16,64,128]{2,1,0:T(8,128)(2,1)S(1)}, bf16[16,64,128]{2,1,0:T(8,128)(2,1)S(1)}, u32[]{:S(2)}, u32[]{:S(2)}) %collective-permute-start.20) | collective-permute-done | bytes 262176 | tf_op jit(solution)/shard_map/ppermute | solution.py:17
  98.2 4.6 %level_2.1 = (bf16[2,64,128]{2,1,0:T(8,128)(2,1)}, bf16[16,64,128]{2,1,0:T(8,128)(2,1)}) custom-call(s32[80]{0:T(128)} %pad_add_fusion.plan, bf16[64,64,128]{2,1,0:T(8,128)(2,1)} %copy-done, bf16[64,64,128]{2,1,0:T(8,128)(2,1)} %copy-done.1, bf16[64,64,128]{2,1,0:T(8,128)(2,1)} %copy-done.2, ...), custom_call_target="tpu_custom_call", output_to_operand_aliasing={{1}: (8, {})} | custom-call | tf_op jit(solution)/shard_map/level_2/pallas_call | solution.py:105
  125.7 7.1 %collective-permute-done.30 = bf16[16,64,128]{2,1,0:T(8,128)(2,1)S(1)} collective-permute-done((bf16[16,64,128]{2,1,0:T(8,128)(2,1)S(1)}, bf16[16,64,128]{2,1,0:T(8,128)(2,1)S(1)}, u32[]{:S(2)}, u32[]{:S(2)}) %collective-permute-start.30) | collective-permute-done | bytes 262176 | tf_op jit(solution)/shard_map/ppermute | solution.py:17
  132.9 4.7 %collective-permute-done.31 = bf16[16,64,128]{2,1,0:T(8,128)(2,1)S(1)} collective-permute-done((bf16[16,64,128]{2,1,0:T(8,128)(2,1)S(1)}, bf16[16,64,128]{2,1,0:T(8,128)(2,1)S(1)}, u32[]{:S(2)}, u32[]{:S(2)}) %collective-permute-start.31) | collective-permute-done | bytes 262176 | tf_op jit(solution)/shard_map/ppermute | solution.py:17
  143.2 4.7 %level_3.1 = (bf16[2,64,128]{2,1,0:T(8,128)(2,1)}, bf16[16,64,128]{2,1,0:T(8,128)(2,1)}) custom-call(s32[80]{0:T(128)} %pad_add_fusion.plan, bf16[64,64,128]{2,1,0:T(8,128)(2,1)} %copy-done, bf16[64,64,128]{2,1,0:T(8,128)(2,1)} %copy-done.1, bf16[64,64,128]{2,1,0:T(8,128)(2,1)} %copy-done.2, ...), custom_call_target="tpu_custom_call", output_to_operand_aliasing={{1}: (10, {})} | custom-call | tf_op jit(solution)/shard_map/level_3/pallas_call | solution.py:105
  158.4 11.1 %collective-permute-start.39 = (bf16[2,64,128]{2,1,0:T(8,128)(2,1)}, bf16[2,64,128]{2,1,0:T(8,128)(2,1)S(1)}, u32[]{:S(2)}, u32[]{:S(2)}) collective-permute-start(bf16[2,64,128]{2,1,0:T(8,128)(2,1)} %get-tuple-element.26), channel_id=1, source_target_pairs={{0,56},{4,60},{8,48},{12,52},{16,40},{20,44},{24,32},{28,36},{32,2... | collective-permute-start | bytes 98312 | tf_op jit(solution)/shard_map/ppermute | solution.py:17
  176.9 4.5 %collective-permute-done.41 = bf16[16,64,128]{2,1,0:T(8,128)(2,1)S(1)} collective-permute-done((bf16[16,64,128]{2,1,0:T(8,128)(2,1)S(1)}, bf16[16,64,128]{2,1,0:T(8,128)(2,1)S(1)}, u32[]{:S(2)}, u32[]{:S(2)}) %collective-permute-start.41) | collective-permute-done | bytes 262176 | tf_op jit(solution)/shard_map/ppermute | solution.py:17
  181.4 4.8 %collective-permute-done.42 = bf16[16,64,128]{2,1,0:T(8,128)(2,1)S(1)} collective-permute-done((bf16[16,64,128]{2,1,0:T(8,128)(2,1)S(1)}, bf16[16,64,128]{2,1,0:T(8,128)(2,1)S(1)}, u32[]{:S(2)}, u32[]{:S(2)}) %collective-permute-start.42) | collective-permute-done | bytes 262176 | tf_op jit(solution)/shard_map/ppermute | solution.py:17
  191.8 4.7 %level_4.1 = (bf16[2,64,128]{2,1,0:T(8,128)(2,1)}, bf16[16,64,128]{2,1,0:T(8,128)(2,1)}) custom-call(s32[80]{0:T(128)} %pad_add_fusion.plan, bf16[64,64,128]{2,1,0:T(8,128)(2,1)} %copy-done, bf16[64,64,128]{2,1,0:T(8,128)(2,1)} %copy-done.1, bf16[64,64,128]{2,1,0:T(8,128)(2,1)} %copy-done.2, ...), custom_call_target="tpu_custom_call", output_to_operand_aliasing={{1}: (12, {})} | custom-call | tf_op jit(solution)/shard_map/level_4/pallas_call | solution.py:105
  219.6 7.8 %collective-permute-done.52 = bf16[16,64,128]{2,1,0:T(8,128)(2,1)S(1)} collective-permute-done((bf16[16,64,128]{2,1,0:T(8,128)(2,1)S(1)}, bf16[16,64,128]{2,1,0:T(8,128)(2,1)S(1)}, u32[]{:S(2)}, u32[]{:S(2)}) %collective-permute-start.52) | collective-permute-done | bytes 262176 | tf_op jit(solution)/shard_map/ppermute | solution.py:17
  227.4 4.1 %collective-permute-done.53 = bf16[16,64,128]{2,1,0:T(8,128)(2,1)S(1)} collective-permute-done((bf16[16,64,128]{2,1,0:T(8,128)(2,1)S(1)}, bf16[16,64,128]{2,1,0:T(8,128)(2,1)S(1)}, u32[]{:S(2)}, u32[]{:S(2)}) %collective-permute-start.53) | collective-permute-done | bytes 262176 | tf_op jit(solution)/shard_map/ppermute | solution.py:17
  237.1 4.7 %level_5.1 = (bf16[2,64,128]{2,1,0:T(8,128)(2,1)}, bf16[16,64,128]{2,1,0:T(8,128)(2,1)}) custom-call(s32[80]{0:T(128)} %pad_add_fusion.plan, bf16[64,64,128]{2,1,0:T(8,128)(2,1)} %copy-done, bf16[64,64,128]{2,1,0:T(8,128)(2,1)} %copy-done.1, bf16[64,64,128]{2,1,0:T(8,128)(2,1)} %copy-done.2, ...), custom_call_target="tpu_custom_call", output_to_operand_aliasing={{1}: (14, {})} | custom-call | tf_op jit(solution)/shard_map/level_5/pallas_call | solution.py:105
  262.8 5.0 %collective-permute-done.63 = bf16[16,64,128]{2,1,0:T(8,128)(2,1)S(1)} collective-permute-done((bf16[16,64,128]{2,1,0:T(8,128)(2,1)S(1)}, bf16[16,64,128]{2,1,0:T(8,128)(2,1)S(1)}, u32[]{:S(2)}, u32[]{:S(2)}) %collective-permute-start.63) | collective-permute-done | bytes 262176 | tf_op jit(solution)/shard_map/ppermute | solution.py:17
  267.8 4.3 %collective-permute-done.64 = bf16[16,64,128]{2,1,0:T(8,128)(2,1)S(1)} collective-permute-done((bf16[16,64,128]{2,1,0:T(8,128)(2,1)S(1)}, bf16[16,64,128]{2,1,0:T(8,128)(2,1)S(1)}, u32[]{:S(2)}, u32[]{:S(2)}) %collective-permute-start.64) | collective-permute-done | bytes 262176 | tf_op jit(solution)/shard_map/ppermute | solution.py:17
  277.7 4.7 %level_6.1 = (bf16[2,64,128]{2,1,0:T(8,128)(2,1)}, bf16[16,64,128]{2,1,0:T(8,128)(2,1)}) custom-call(s32[80]{0:T(128)} %pad_add_fusion.plan, bf16[64,64,128]{2,1,0:T(8,128)(2,1)} %copy-done, bf16[64,64,128]{2,1,0:T(8,128)(2,1)} %copy-done.1, bf16[64,64,128]{2,1,0:T(8,128)(2,1)} %copy-done.2, ...), custom_call_target="tpu_custom_call", output_to_operand_aliasing={{1}: (16, {})} | custom-call | tf_op jit(solution)/shard_map/level_6/pallas_call | solution.py:105
  305.2 7.8 %collective-permute-done.74 = bf16[16,64,128]{2,1,0:T(8,128)(2,1)S(1)} collective-permute-done((bf16[16,64,128]{2,1,0:T(8,128)(2,1)S(1)}, bf16[16,64,128]{2,1,0:T(8,128)(2,1)S(1)}, u32[]{:S(2)}, u32[]{:S(2)}) %collective-permute-start.74) | collective-permute-done | bytes 262176 | tf_op jit(solution)/shard_map/ppermute | solution.py:17
  313.0 4.1 %collective-permute-done.75 = bf16[16,64,128]{2,1,0:T(8,128)(2,1)S(1)} collective-permute-done((bf16[16,64,128]{2,1,0:T(8,128)(2,1)S(1)}, bf16[16,64,128]{2,1,0:T(8,128)(2,1)S(1)}, u32[]{:S(2)}, u32[]{:S(2)}) %collective-permute-start.75) | collective-permute-done | bytes 262176 | tf_op jit(solution)/shard_map/ppermute | solution.py:17
  322.7 4.7 %level_7.1 = (bf16[2,64,128]{2,1,0:T(8,128)(2,1)}, bf16[16,64,128]{2,1,0:T(8,128)(2,1)}) custom-call(s32[80]{0:T(128)} %pad_add_fusion.plan, bf16[64,64,128]{2,1,0:T(8,128)(2,1)} %copy-done, bf16[64,64,128]{2,1,0:T(8,128)(2,1)} %copy-done.1, bf16[64,64,128]{2,1,0:T(8,128)(2,1)} %copy-done.2, ...), custom_call_target="tpu_custom_call", output_to_operand_aliasing={{1}: (18, {})} | custom-call | tf_op jit(solution)/shard_map/level_7/pallas_call | solution.py:105
  (259 shorter events, 191.4 us)
Async XLA Ops:
  6.5 50.6 %all-gather.3.cloned.1.call-start = ((), (), s32[]{:S(2)}) async-start(), calls=%async_computation | async-start | bytes 2621440 | tf_op jit(solution)/shard_map/all_gather | solution.py:139
  14.1 12.2 %collective-permute-start = (bf16[2,64,128]{2,1,0:T(8,128)(2,1)}, bf16[2,64,128]{2,1,0:T(8,128)(2,1)S(1)}, u32[]{:S(2)}, u32[]{:S(2)}) collective-permute-start(bf16[2,64,128]{2,1,0:T(8,128)(2,1)} %get-tuple-element.20), channel_id=1, source_target_pairs={{0,8},{4,12},{8,0},{12,4},{16,24},{20,28},{24,16},{28,20},{32,40},... | collective-permute-start | bytes 98312 | tf_op jit(solution)/shard_map/ppermute | solution.py:17
  16.6 13.8 %collective-permute-start.1 = (bf16[2,64,128]{2,1,0:T(8,128)(2,1)}, bf16[2,64,128]{2,1,0:T(8,128)(2,1)S(1)}, u32[]{:S(2)}, u32[]{:S(2)}) collective-permute-start(bf16[2,64,128]{2,1,0:T(8,128)(2,1)} %get-tuple-element.20), channel_id=1, source_target_pairs={{0,16},{4,20},{8,24},{12,28},{16,0},{20,4},{24,8},{28,12},{32,48},... | collective-permute-start | bytes 98312 | tf_op jit(solution)/shard_map/ppermute | solution.py:17
  19.6 10.9 %collective-permute-start.2 = (bf16[2,64,128]{2,1,0:T(8,128)(2,1)}, bf16[2,64,128]{2,1,0:T(8,128)(2,1)S(1)}, u32[]{:S(2)}, u32[]{:S(2)}) collective-permute-start(bf16[2,64,128]{2,1,0:T(8,128)(2,1)} %get-tuple-element.20), channel_id=1, source_target_pairs={{0,24},{4,28},{8,16},{12,20},{16,8},{20,12},{24,0},{28,4},{32,56},... | collective-permute-start | bytes 98312 | tf_op jit(solution)/shard_map/ppermute | solution.py:17
  19.6 11.0 %collective-permute-start.3 = (bf16[2,64,128]{2,1,0:T(8,128)(2,1)}, bf16[2,64,128]{2,1,0:T(8,128)(2,1)S(1)}, u32[]{:S(2)}, u32[]{:S(2)}) collective-permute-start(bf16[2,64,128]{2,1,0:T(8,128)(2,1)} %get-tuple-element.20), channel_id=1, source_target_pairs={{0,32},{4,36},{8,40},{12,44},{16,48},{20,52},{24,56},{28,60},{32,0... | collective-permute-start | bytes 98312 | tf_op jit(solution)/shard_map/ppermute | solution.py:17
  36.5 11.2 %collective-permute-start.8 = (bf16[16,64,128]{2,1,0:T(8,128)(2,1)S(1)}, bf16[16,64,128]{2,1,0:T(8,128)(2,1)S(1)}, u32[]{:S(2)}, u32[]{:S(2)}) collective-permute-start(bf16[16,64,128]{2,1,0:T(8,128)(2,1)S(1)} %get-tuple-element.131), channel_id=1, source_target_pairs={{0,128},{4,132},{8,136},{12,140},{16,144},{20,148},{24,152},{28,15... | collective-permute-start | bytes 786440 | tf_op jit(solution)/shard_map/ppermute | solution.py:17
  39.1 13.4 %collective-permute-start.9 = (bf16[16,64,128]{2,1,0:T(8,128)(2,1)S(1)}, bf16[16,64,128]{2,1,0:T(8,128)(2,1)S(1)}, u32[]{:S(2)}, u32[]{:S(2)}) collective-permute-start(bf16[16,64,128]{2,1,0:T(8,128)(2,1)S(1)} %get-tuple-element.131), channel_id=1, source_target_pairs={{0,192},{4,196},{8,200},{12,204},{16,208},{20,212},{24,216},{28,22... | collective-permute-start | bytes 786440 | tf_op jit(solution)/shard_map/ppermute | solution.py:17
  79.4 13.3 %collective-permute-start.20 = (bf16[16,64,128]{2,1,0:T(8,128)(2,1)S(1)}, bf16[16,64,128]{2,1,0:T(8,128)(2,1)S(1)}, u32[]{:S(2)}, u32[]{:S(2)}) collective-permute-start(bf16[16,64,128]{2,1,0:T(8,128)(2,1)S(1)} %get-tuple-element.115), channel_id=1, source_target_pairs={{0,192},{4,196},{8,200},{12,204},{16,208},{20,212},{24,216},{28,22... | collective-permute-start | bytes 786440 | tf_op jit(solution)/shard_map/ppermute | solution.py:17
  105.5 10.4 %collective-permute-start.23 = (bf16[2,64,128]{2,1,0:T(8,128)(2,1)}, bf16[2,64,128]{2,1,0:T(8,128)(2,1)S(1)}, u32[]{:S(2)}, u32[]{:S(2)}) collective-permute-start(bf16[2,64,128]{2,1,0:T(8,128)(2,1)} %get-tuple-element.24), channel_id=1, source_target_pairs={{0,16},{4,20},{8,24},{12,28},{16,0},{20,4},{24,8},{28,12},{32,48},... | collective-permute-start | bytes 98312 | tf_op jit(solution)/shard_map/ppermute | solution.py:17
  120.4 12.4 %collective-permute-start.30 = (bf16[16,64,128]{2,1,0:T(8,128)(2,1)S(1)}, bf16[16,64,128]{2,1,0:T(8,128)(2,1)S(1)}, u32[]{:S(2)}, u32[]{:S(2)}) collective-permute-start(bf16[16,64,128]{2,1,0:T(8,128)(2,1)S(1)} %get-tuple-element.99), channel_id=1, source_target_pairs={{0,128},{4,132},{8,136},{12,140},{16,144},{20,148},{24,152},{28,15... | collective-permute-start | bytes 786440 | tf_op jit(solution)/shard_map/ppermute | solution.py:17
  124.2 13.4 %collective-permute-start.31 = (bf16[16,64,128]{2,1,0:T(8,128)(2,1)S(1)}, bf16[16,64,128]{2,1,0:T(8,128)(2,1)S(1)}, u32[]{:S(2)}, u32[]{:S(2)}) collective-permute-start(bf16[16,64,128]{2,1,0:T(8,128)(2,1)S(1)} %get-tuple-element.99), channel_id=1, source_target_pairs={{0,192},{4,196},{8,200},{12,204},{16,208},{20,212},{24,216},{28,22... | collective-permute-start | bytes 786440 | tf_op jit(solution)/shard_map/ppermute | solution.py:17
  150.9 18.6 %collective-permute-start.35 = (bf16[2,64,128]{2,1,0:T(8,128)(2,1)}, bf16[2,64,128]{2,1,0:T(8,128)(2,1)S(1)}, u32[]{:S(2)}, u32[]{:S(2)}) collective-permute-start(bf16[2,64,128]{2,1,0:T(8,128)(2,1)} %get-tuple-element.26), channel_id=1, source_target_pairs={{0,24},{4,28},{8,16},{12,20},{16,8},{20,12},{24,0},{28,4},{32,56},... | collective-permute-start | bytes 98312 | tf_op jit(solution)/shard_map/ppermute | solution.py:17
  152.5 17.0 %collective-permute-start.36 = (bf16[2,64,128]{2,1,0:T(8,128)(2,1)}, bf16[2,64,128]{2,1,0:T(8,128)(2,1)S(1)}, u32[]{:S(2)}, u32[]{:S(2)}) collective-permute-start(bf16[2,64,128]{2,1,0:T(8,128)(2,1)} %get-tuple-element.26), channel_id=1, source_target_pairs={{0,32},{4,36},{8,40},{12,44},{16,48},{20,52},{24,56},{28,60},{32,0... | collective-permute-start | bytes 98312 | tf_op jit(solution)/shard_map/ppermute | solution.py:17
  154.4 15.3 %collective-permute-start.37 = (bf16[2,64,128]{2,1,0:T(8,128)(2,1)}, bf16[2,64,128]{2,1,0:T(8,128)(2,1)S(1)}, u32[]{:S(2)}, u32[]{:S(2)}) collective-permute-start(bf16[2,64,128]{2,1,0:T(8,128)(2,1)} %get-tuple-element.26), channel_id=1, source_target_pairs={{0,40},{4,44},{8,32},{12,36},{16,56},{20,60},{24,48},{28,52},{32,8... | collective-permute-start | bytes 98312 | tf_op jit(solution)/shard_map/ppermute | solution.py:17
  157.3 12.4 %collective-permute-start.38 = (bf16[2,64,128]{2,1,0:T(8,128)(2,1)}, bf16[2,64,128]{2,1,0:T(8,128)(2,1)S(1)}, u32[]{:S(2)}, u32[]{:S(2)}) collective-permute-start(bf16[2,64,128]{2,1,0:T(8,128)(2,1)} %get-tuple-element.26), channel_id=1, source_target_pairs={{0,48},{4,52},{8,56},{12,60},{16,32},{20,36},{24,40},{28,44},{32,1... | collective-permute-start | bytes 98312 | tf_op jit(solution)/shard_map/ppermute | solution.py:17
  158.4 13.1 %collective-permute-start.39 = (bf16[2,64,128]{2,1,0:T(8,128)(2,1)}, bf16[2,64,128]{2,1,0:T(8,128)(2,1)S(1)}, u32[]{:S(2)}, u32[]{:S(2)}) collective-permute-start(bf16[2,64,128]{2,1,0:T(8,128)(2,1)} %get-tuple-element.26), channel_id=1, source_target_pairs={{0,56},{4,60},{8,48},{12,52},{16,40},{20,44},{24,32},{28,36},{32,2... | collective-permute-start | bytes 98312 | tf_op jit(solution)/shard_map/ppermute | solution.py:17
  172.8 13.4 %collective-permute-start.42 = (bf16[16,64,128]{2,1,0:T(8,128)(2,1)S(1)}, bf16[16,64,128]{2,1,0:T(8,128)(2,1)S(1)}, u32[]{:S(2)}, u32[]{:S(2)}) collective-permute-start(bf16[16,64,128]{2,1,0:T(8,128)(2,1)S(1)} %get-tuple-element.83), channel_id=1, source_target_pairs={{0,192},{4,196},{8,200},{12,204},{16,208},{20,212},{24,216},{28,22... | collective-permute-start | bytes 786440 | tf_op jit(solution)/shard_map/ppermute | solution.py:17
  196.4 10.2 %collective-permute-start.44 = (bf16[2,64,128]{2,1,0:T(8,128)(2,1)}, bf16[2,64,128]{2,1,0:T(8,128)(2,1)S(1)}, u32[]{:S(2)}, u32[]{:S(2)}) collective-permute-start(bf16[2,64,128]{2,1,0:T(8,128)(2,1)} %get-tuple-element.28), channel_id=1, source_target_pairs={{0,8},{4,12},{8,0},{12,4},{16,24},{20,28},{24,16},{28,20},{32,40},... | collective-permute-start | bytes 98312 | tf_op jit(solution)/shard_map/ppermute | solution.py:17
  214.3 13.0 %collective-permute-start.52 = (bf16[16,64,128]{2,1,0:T(8,128)(2,1)S(1)}, bf16[16,64,128]{2,1,0:T(8,128)(2,1)S(1)}, u32[]{:S(2)}, u32[]{:S(2)}) collective-permute-start(bf16[16,64,128]{2,1,0:T(8,128)(2,1)S(1)} %get-tuple-element.67), channel_id=1, source_target_pairs={{0,128},{4,132},{8,136},{12,140},{16,144},{20,148},{24,152},{28,15... | collective-permute-start | bytes 786440 | tf_op jit(solution)/shard_map/ppermute | solution.py:17
  218.2 13.4 %collective-permute-start.53 = (bf16[16,64,128]{2,1,0:T(8,128)(2,1)S(1)}, bf16[16,64,128]{2,1,0:T(8,128)(2,1)S(1)}, u32[]{:S(2)}, u32[]{:S(2)}) collective-permute-start(bf16[16,64,128]{2,1,0:T(8,128)(2,1)S(1)} %get-tuple-element.67), channel_id=1, source_target_pairs={{0,192},{4,196},{8,200},{12,204},{16,208},{20,212},{24,216},{28,22... | collective-permute-start | bytes 786440 | tf_op jit(solution)/shard_map/ppermute | solution.py:17
  257.6 10.2 %collective-permute-start.63 = (bf16[16,64,128]{2,1,0:T(8,128)(2,1)S(1)}, bf16[16,64,128]{2,1,0:T(8,128)(2,1)S(1)}, u32[]{:S(2)}, u32[]{:S(2)}) collective-permute-start(bf16[16,64,128]{2,1,0:T(8,128)(2,1)S(1)} %get-tuple-element.51), channel_id=1, source_target_pairs={{0,128},{4,132},{8,136},{12,140},{16,144},{20,148},{24,152},{28,15... | collective-permute-start | bytes 786440 | tf_op jit(solution)/shard_map/ppermute | solution.py:17
  258.7 13.4 %collective-permute-start.64 = (bf16[16,64,128]{2,1,0:T(8,128)(2,1)S(1)}, bf16[16,64,128]{2,1,0:T(8,128)(2,1)S(1)}, u32[]{:S(2)}, u32[]{:S(2)}) collective-permute-start(bf16[16,64,128]{2,1,0:T(8,128)(2,1)S(1)} %get-tuple-element.51), channel_id=1, source_target_pairs={{0,192},{4,196},{8,200},{12,204},{16,208},{20,212},{24,216},{28,22... | collective-permute-start | bytes 786440 | tf_op jit(solution)/shard_map/ppermute | solution.py:17
  299.9 13.0 %collective-permute-start.74 = (bf16[16,64,128]{2,1,0:T(8,128)(2,1)S(1)}, bf16[16,64,128]{2,1,0:T(8,128)(2,1)S(1)}, u32[]{:S(2)}, u32[]{:S(2)}) collective-permute-start(bf16[16,64,128]{2,1,0:T(8,128)(2,1)S(1)} %get-tuple-element.35), channel_id=1, source_target_pairs={{0,128},{4,132},{8,136},{12,140},{16,144},{20,148},{24,152},{28,15... | collective-permute-start | bytes 786440 | tf_op jit(solution)/shard_map/ppermute | solution.py:17
  303.7 13.4 %collective-permute-start.75 = (bf16[16,64,128]{2,1,0:T(8,128)(2,1)S(1)}, bf16[16,64,128]{2,1,0:T(8,128)(2,1)S(1)}, u32[]{:S(2)}, u32[]{:S(2)}) collective-permute-start(bf16[16,64,128]{2,1,0:T(8,128)(2,1)S(1)} %get-tuple-element.35), channel_id=1, source_target_pairs={{0,192},{4,196},{8,200},{12,204},{16,208},{20,212},{24,216},{28,22... | collective-permute-start | bytes 786440 | tf_op jit(solution)/shard_map/ppermute | solution.py:17
  (68 other events, 408.1 us)
Sparse Core Ops, SparseCore 0:
  9.2 37.1 all-gather.2
